TPU v7x, 512 devices: a whole 4x4x16 slice. The times are simulated.
512 devices in a mesh: outer: 16 (over y, x), inner: 32 (over z, core).
Axes of the slice: x: 4, y: 4, z: 16, core: 2. Of those that a mesh axis runs over, the one named last changes fastest.
Arguments:
- query_states: bfloat16 [65536, 2048], P(('outer', 'inner')), may hold values from -400 to 400
- key_states: bfloat16 [65536, 2048], P(('outer', 'inner')), may hold values from -13 to 13
- value_states: bfloat16 [65536, 2048], P(('outer', 'inner')), may hold values from -27 to 27
Outputs:
- attention_out: bfloat16 [65536, 2048], P(('outer', 'inner'))
All inputs are finite; a program needn't handle non-finite values.
Results may differ from a plain program's by a relative error of at most 0.0038.
Values may be sent and summed in bfloat16 or wider, within the bound.
A program may use at most 64 MiB of HBM per device.

v0:
```python
import math

import jax
import jax.numpy as jnp
from jax import lax
from jax.experimental import pallas as pl
from jax.experimental.pallas import tpu as pltpu
from jax.sharding import PartitionSpec as P

HEADS = 16
HALF = HEADS // 2
DIM = 128
LEAF = 128
CHIPS = 16
CHUNKS = 4
PER = HALF // CHUNKS
SCALE = 1.0 / math.sqrt(DIM)
SCALE2 = SCALE * math.log2(math.e)
MESH = pl.DeviceIdType.MESH
BF = jnp.bfloat16
F32 = jnp.float32


def nn(a, b):
    return lax.dot_general(a, b, (((1,), (0,)), ((), ())), preferred_element_type=F32)


def nt(a, b):
    return lax.dot_general(a, b, (((1,), (1,)), ((), ())), preferred_element_type=F32)


def grid_of(rows, columns):
    return (
        lax.broadcasted_iota(jnp.int32, (rows, columns), 0),
        lax.broadcasted_iota(jnp.int32, (rows, columns), 1),
    )


def halving(rows):
    i, j = grid_of(rows // 2, rows)
    return jnp.where((j >> 1) == i, 0.5, 0.0).astype(BF)


def halving_spread(rows, level):
    i, j = grid_of(rows, rows)
    first = (j & ((1 << (level - 1)) - 1)) == 0
    return jnp.where(((i >> level) == (j >> level)) & first, 0.5, 0.0).astype(BF)


def with_ones(values):
    return jnp.concatenate([values, jnp.ones_like(values)], axis=1)


def attend(scores, values):
    peak = jnp.max(scores[0], axis=1, keepdims=True)
    for s in scores[1:]:
        peak = jnp.maximum(peak, jnp.max(s, axis=1, keepdims=True))
    total = None
    for s, v in zip(scores, values):
        w = jnp.exp2((s - peak) * SCALE2).astype(BF)
        part = nn(w, with_ones(v))
        total = part if total is None else total + part
    den = total[:, DIM:]
    return total[:, :DIM] / den, peak, jnp.log(den)


def split3(x):
    high = x.astype(BF)
    rest = x - high.astype(F32)
    mid = rest.astype(BF)
    low = (rest - mid.astype(F32)).astype(BF)
    return jnp.concatenate([high, mid, low], axis=1)


def kernel(
    q_in, k_in, v_in, out,
    full, near, kv1_s, kv1_r, far_s, far_r, kv3, kv4_s, kv5_s, kv6_s, kv4_r, kv5_r, kv6_r,
    q_up, res_s, stat_s, res_r, stat_r, near_o, near_m, near_l, done,
    load_sem, own_sem, near_ss, near_rs, far_ss, far_rs, kv1_ss, kv1_rs, up_ss, up_rs,
    res_ss, res_rs, stat_ss, stat_rs, out_ls, out_ss, out_rs,
):
    o = lax.axis_index("outer")
    n = lax.axis_index("inner")
    c = n % 2
    z = n // 2
    half = z // 8
    zl = z % 8
    other = 1 - c
    differ = (half + c) % 2
    mate = (o, 2 * z + other)
    zs = z + 1 - 2 * (z % 2)
    o1 = o + 1 - 2 * (o % 2)
    o2 = o + 2 - 4 * ((o // 2) % 2)
    o3 = o2 + 1 - 2 * (o2 % 2)
    inputs = (q_in, k_in, v_in)

    def remote(src, dst, ss, rs, device):
        return pltpu.make_async_remote_copy(
            src_ref=src, dst_ref=dst, send_sem=ss, recv_sem=rs, device_id=device, device_id_type=MESH
        )

    loads = [pltpu.make_async_copy(inputs[i], full.at[i], load_sem.at[i]) for i in range(3)]
    for copy in loads:
        copy.start()

    barrier = pltpu.get_barrier_semaphore()

    def greet(i, carry):
        d = 16 * c + i

        @pl.when(d != n)
        def _():
            pl.semaphore_signal(barrier, inc=1, device_id=(o, d), device_id_type=MESH)

        return carry

    lax.fori_loop(0, 16, greet, 0)
    pl.semaphore_signal(barrier, inc=1, device_id=mate, device_id_type=MESH)
    for cc in range(2):
        for device in ((o, 2 * zs + cc), (o1, 2 * z + cc), (o2, 2 * z + cc), (o3, 2 * z + cc)):
            pl.semaphore_signal(barrier, inc=1, device_id=device, device_id_type=MESH)

    own = [
        pltpu.make_async_copy(
            inputs[i].at[:, pl.ds(1024 * c, 1024)], near.at[i, pl.ds(128 * c, 128), :], own_sem.at[i]
        )
        for i in range(3)
    ]
    for copy in own:
        copy.start()

    for copy in loads:
        copy.wait()

    half128 = halving(128)
    half64 = halving(64)

    def pool(i, carry):
        at = pl.ds(pl.multiple_of(i * 512, 512), 512)
        one = [nn(half128, full[a, :, at]).astype(BF) for a in range(3)]
        two = [nn(half64, x).astype(BF) for x in one]
        for u in range(4):
            h = i * 4 + u
            cut = slice(u * DIM, (u + 1) * DIM)
            kv1_s[h] = jnp.concatenate([one[1][:, cut], one[2][:, cut]], axis=1)
            far_s[h] = jnp.concatenate([two[0][:, cut], two[1][:, cut], two[2][:, cut]], axis=1)
        return carry

    lax.fori_loop(0, 4, pool, 0)

    pl.semaphore_wait(barrier, 24 + differ)

    mine = zl * 2 + c

    @pl.when(differ == 0)
    def _():
        pltpu.make_async_copy(far_s.at[z], far_r.at[mine], far_rs.at[mine]).start()

    @pl.when(differ == 1)
    def _():
        remote(far_s.at[z], far_r.at[mine], far_ss.at[0], far_rs.at[mine], mate).start()

    def far_copy(k):
        step = (k + 1) // 2
        zz = (z + 16 + step * (2 * (k % 2) - 1)) % 16
        return remote(far_s.at[zz], far_r.at[mine], far_ss.at[k], far_rs.at[mine], (o, 2 * zz + half))

    def send_far(k, carry):
        far_copy(k).start()
        return carry

    lax.fori_loop(1, 16, send_far, 0)

    near_copies = [
        remote(
            inputs[i].at[:, pl.ds(1024 * other, 1024)], near.at[i, pl.ds(128 * c, 128), :],
            near_ss.at[i], near_rs.at[i], mate,
        )
        for i in range(3)
    ]
    for copy in near_copies:
        copy.start()

    def wait_far(s, carry):
        remote(far_s.at[0], far_r.at[s], far_ss.at[0], far_rs.at[s], mate).wait_recv()
        return carry

    lax.fori_loop(0, 16, wait_far, 0)

    def kv1_copy(q, cc):
        return remote(
            kv1_s.at[pl.ds(HALF * cc + PER * q, PER)],
            kv1_r.at[pl.ds(PER * q, PER), pl.ds(64 * c, 64), :],
            kv1_ss.at[cc, q], kv1_rs.at[c, q], (o, 2 * zs + cc),
        )

    def send_kv1(q, carry):
        for cc in range(2):
            kv1_copy(q, cc).start()
        return carry

    lax.fori_loop(0, CHUNKS, send_kv1, 0)

    kv2 = [far_r[pl.ds(4 * g, 4), :, DIM:].reshape(128, 2 * DIM) for g in range(4)]
    for g in range(4):
        kv3[pl.ds(64 * g, 64), :] = nn(half128, kv2[g]).astype(BF)
    for g in range(2):
        kv4_s[pl.ds(64 * g, 64), :] = nn(half128, kv3[pl.ds(128 * g, 128), :]).astype(BF)
    up = [remote(kv4_s, kv4_r, up_ss.at[0], up_rs.at[0], mate)]
    up[0].start()
    kv5 = nn(half128, kv4_s[...]).astype(BF)
    kv5_s[...] = kv5
    for cc in range(2):
        copy = remote(kv5_s, kv5_r.at[c], up_ss.at[1 + cc], up_rs.at[1 + c], (o1, 2 * z + cc))
        copy.start()
        up.append(copy)
    kv6_s[...] = nn(half64, kv5).astype(BF)
    slot = 2 * (o % 2) + c
    for k, line in enumerate((o2, o3)):
        for cc in range(2):
            copy = remote(
                kv6_s, kv6_r.at[slot], up_ss.at[3 + 2 * k + cc], up_rs.at[3 + slot], (line, 2 * z + cc)
            )
            copy.start()
            up.append(copy)

    spreads = [halving_spread(128, level) for level in range(1, 5)]

    def pool_queries(g, carry):
        x = far_r[pl.ds(4 * g, 4), :, :DIM].reshape(128, DIM)
        for level in range(4):
            x = nn(spreads[level], x).astype(BF)
            q_up[level, g] = x
        return carry

    lax.fori_loop(0, 4, pool_queries, 0)

    remote(kv4_s, kv4_r, up_ss.at[0], up_rs.at[0], mate).wait_recv()
    for cc in range(2):
        remote(kv5_s, kv5_r.at[cc], up_ss.at[1], up_rs.at[1 + cc], mate).wait_recv()
    for s in range(4):
        remote(kv6_s, kv6_r.at[s], up_ss.at[3], up_rs.at[3 + s], mate).wait_recv()

    eye_i, eye_j = grid_of(128, 128)
    eye = eye_i == eye_j

    def result_copies(i):
        device = (o, 2 * (8 * c + i) + half)
        return (
            remote(res_s.at[i], res_r.at[zl], res_ss.at[i], res_rs.at[zl], device),
            remote(stat_s.at[i // 2], stat_r.at[zl], stat_ss.at[i], stat_rs.at[zl], device),
        )

    def is_self(i):
        return 8 * c + i + 16 * differ == z

    def far_attention(g, carry):
        q2 = far_r[pl.ds(4 * g, 4), :, :DIM].reshape(128, DIM)
        g1 = g + 1 - 2 * (g % 2)
        keys = [
            far_r[pl.ds(4 * g1, 4), :, DIM:].reshape(128, 2 * DIM),
            kv3[pl.ds(pl.multiple_of(128 * (1 - g // 2), 128), 128), :],
            kv4_r[...],
            kv5_r[...].reshape(128, 2 * DIM),
            kv6_r[...].reshape(128, 2 * DIM),
        ]
        queries = [q2] + [q_up[level, g] for level in range(4)]
        scores = [nt(q, kv[:, :DIM]) for q, kv in zip(queries, keys)]
        result, peak, total = attend(scores, [kv[:, DIM:] for kv in keys])
        res_s[2 * g] = result[:64].astype(BF)
        res_s[2 * g + 1] = result[64:].astype(BF)
        stat_s[g, 0:1, :] = jnp.sum(jnp.where(eye, peak, 0.0), axis=0, keepdims=True)
        stat_s[g, 1:2, :] = jnp.sum(jnp.where(eye, total, 0.0), axis=0, keepdims=True)
        for u in range(2):
            i = 2 * g + u

            @pl.when(is_self(i))
            def _():
                pltpu.make_async_copy(res_s.at[i], res_r.at[zl], res_rs.at[zl]).start()
                pltpu.make_async_copy(stat_s.at[g], stat_r.at[zl], stat_rs.at[zl]).start()

            @pl.when(jnp.logical_not(is_self(i)))
            def _():
                for copy in result_copies(i):
                    copy.start()

        return carry

    lax.fori_loop(0, 4, far_attention, 0)

    for copy in own:
        copy.wait()
    for i in range(3):
        remote(
            inputs[i].at[:, pl.ds(1024 * other, 1024)], near.at[i, pl.ds(128 * other, 128), :],
            near_ss.at[i], near_rs.at[i], mate,
        ).wait_recv()
    pairs = halving_spread(256, 1)

    def near_attention(q, carry):
        for cc in range(2):
            remote(
                kv1_s.at[pl.ds(0, PER)], kv1_r.at[pl.ds(PER * q, PER), pl.ds(64 * cc, 64), :],
                kv1_ss.at[0, q], kv1_rs.at[cc, q], mate,
            ).wait_recv()
        for u in range(PER):
            j = PER * q + u
            at = pl.ds(pl.multiple_of(j * DIM, DIM), DIM)
            x = near[0, :, at]
            x1 = nn(pairs, x).astype(BF)
            kv1 = kv1_r[j]
            scores = [nt(x, near[1, :, at]), nt(x1, kv1[:, :DIM])]
            result, peak, total = attend(scores, [near[2, :, at], kv1[:, DIM:]])
            near_o[j] = result
            near_m[j] = jnp.broadcast_to(peak, (256, DIM))
            near_l[j] = total
        return carry

    lax.fori_loop(0, CHUNKS, near_attention, 0)

    ri, rj = grid_of(256, 64)
    repeat4 = jnp.where((ri >> 2) == rj, 1.0, 0.0).astype(BF)
    si, sj = grid_of(256, DIM)
    pick = jnp.where((si >> 2) + 64 * (z % 2) == sj, 1.0, 0.0).astype(BF)
    pick3 = jnp.concatenate([pick, pick, pick], axis=1)

    def out_copies(j):
        at = pl.ds(pl.multiple_of((HALF * c + j) * DIM, DIM), DIM)
        return (
            pltpu.make_async_copy(done.at[j, pl.ds(128 * c, 128), :], out.at[:, at], out_ls.at[j]),
            remote(done.at[j, pl.ds(128 * other, 128), :], out.at[:, at], out_ss.at[j], out_rs.at[j], mate),
        )

    def merge(q, carry):
        for u in range(2):
            j = 2 * q + u
            remote(res_s.at[0], res_r.at[j], res_ss.at[0], res_rs.at[j], mate).wait_recv()
            remote(stat_s.at[0], stat_r.at[j], stat_ss.at[0], stat_rs.at[j], mate).wait_recv()
            coarse = nn(repeat4, res_r[j])
            peak = nt(pick3, jnp.broadcast_to(split3(stat_r[j, 0:1, :]), (DIM, 3 * DIM)))
            total = nt(pick3, jnp.broadcast_to(split3(stat_r[j, 1:2, :]), (DIM, 3 * DIM)))
            gap = (peak - near_m[j]) * SCALE + (total - near_l[j])
            share = 1.0 / (1.0 + jnp.exp(-gap))
            fine = near_o[j]
            done[j] = (fine + share * (coarse - fine)).astype(BF)
            for copy in out_copies(j):
                copy.start()
        return carry

    lax.fori_loop(0, HALF // 2, merge, 0)

    @pl.when(differ == 1)
    def _():
        remote(far_s.at[z], far_r.at[mine], far_ss.at[0], far_rs.at[mine], mate).wait_send()

    def end_far(k, carry):
        far_copy(k).wait_send()
        return carry

    lax.fori_loop(1, 16, end_far, 0)
    for copy in near_copies:
        copy.wait_send()

    def end_kv1(q, carry):
        for cc in range(2):
            kv1_copy(q, cc).wait_send()
        return carry

    lax.fori_loop(0, CHUNKS, end_kv1, 0)
    for copy in up:
        copy.wait_send()

    def end_results(i, carry):
        @pl.when(jnp.logical_not(is_self(i)))
        def _():
            for copy in result_copies(i):
                copy.wait_send()

        return carry

    lax.fori_loop(0, 8, end_results, 0)

    def end_out(j, carry):
        local, far = out_copies(j)
        local.wait()
        far.wait_send()
        at = pl.ds(pl.multiple_of((HALF * other + j) * DIM, DIM), DIM)
        remote(done.at[j, pl.ds(0, 128), :], out.at[:, at], out_ss.at[j], out_rs.at[j], mate).wait_recv()
        return carry

    lax.fori_loop(0, HALF, end_out, 0)


def body(query_states, key_states, value_states):
    dma = pltpu.SemaphoreType.DMA
    vmem = pltpu.VMEM
    return pl.pallas_call(
        kernel,
        out_shape=jax.ShapeDtypeStruct(query_states.shape, BF),
        in_specs=[pl.BlockSpec(memory_space=pl.ANY)] * 3,
        out_specs=pl.BlockSpec(memory_space=pl.ANY),
        scratch_shapes=[
            vmem((3, LEAF, HEADS * DIM), BF),
            vmem((3, 2 * LEAF, HALF * DIM), BF),
            vmem((HEADS, 64, 2 * DIM), BF),
            vmem((HALF, 128, 2 * DIM), BF),
            vmem((HEADS, 32, 3 * DIM), BF),
            vmem((CHIPS, 32, 3 * DIM), BF),
            vmem((256, 2 * DIM), BF),
            vmem((128, 2 * DIM), BF),
            vmem((64, 2 * DIM), BF),
            vmem((32, 2 * DIM), BF),
            vmem((128, 2 * DIM), BF),
            vmem((2, 64, 2 * DIM), BF),
            vmem((4, 32, 2 * DIM), BF),
            vmem((4, 4, 128, DIM), BF),
            vmem((8, 64, DIM), BF),
            vmem((4, 2, DIM), F32),
            vmem((8, 64, DIM), BF),
            vmem((8, 2, DIM), F32),
            vmem((HALF, 256, DIM), F32),
            vmem((HALF, 256, DIM), F32),
            vmem((HALF, 256, DIM), F32),
            vmem((HALF, 256, DIM), BF),
            dma((3,)), dma((3,)), dma((3,)), dma((3,)),
            dma((16,)), dma((16,)), dma((2, CHUNKS)), dma((2, CHUNKS)), dma((7,)), dma((7,)),
            dma((8,)), dma((8,)), dma((8,)), dma((8,)), dma((8,)), dma((8,)), dma((8,)),
        ],
        compiler_params=pltpu.CompilerParams(
            collective_id=0, has_side_effects=True, vmem_limit_bytes=32 * 1024 * 1024
        ),
        cost_estimate=pl.CostEstimate(flops=600_000_000, bytes_accessed=3_000_000, transcendentals=1_200_000),
        name="tree_attention",
    )(query_states, key_states, value_states)


def solution(mesh):
    placed = P(("outer", "inner"), None)
    return jax.shard_map(body, mesh=mesh, in_specs=(placed,) * 3, out_specs=placed, check_vma=False)
```

profile of v0, /device:TPU:11, one launch (start us, length us, event | category | flops | bytes accessed | tf_op | source)
XLA Modules:
  0.0 64.8 jit_solution(4911001625522330702)
XLA Ops:
  0.0 0.0 copy-start
  0.0 1.0 %copy-done = bf16[128,2048]{1,0:T(8,128)(2,1)S(1)} copy-done((bf16[128,2048]{1,0:T(8,128)(2,1)S(1)}, bf16[128,2048]{1,0:T(8,128)(2,1)}, u32[]{:S(2)}) %copy-start) | copy-done | bytes 524312
  1.0 0.0 copy-start.1
  1.0 1.0 %copy-done.1 = bf16[128,2048]{1,0:T(8,128)(2,1)S(1)} copy-done((bf16[128,2048]{1,0:T(8,128)(2,1)S(1)}, bf16[128,2048]{1,0:T(8,128)(2,1)}, u32[]{:S(2)}) %copy-start.1) | copy-done | bytes 524312
  2.1 0.0 copy-start.2
  2.1 1.0 %copy-done.2 = bf16[128,2048]{1,0:T(8,128)(2,1)S(1)} copy-done((bf16[128,2048]{1,0:T(8,128)(2,1)S(1)}, bf16[128,2048]{1,0:T(8,128)(2,1)}, u32[]{:S(2)}) %copy-start.2) | copy-done | bytes 524312
  3.1 60.9 %tree_attention.1 = bf16[128,2048]{1,0:T(8,128)(2,1)S(1)} custom-call(bf16[128,2048]{1,0:T(8,128)(2,1)S(1)} %copy-done, bf16[128,2048]{1,0:T(8,128)(2,1)S(1)} %copy-done.1, bf16[128,2048]{1,0:T(8,128)(2,1)S(1)} %copy-done.2), custom_call_target="tpu_custom_call" | custom-call | flops 600000000 | bytes 3000000 | tf_op jit(solution)/shard_map/tree_attention/pallas_call | solution.py:397
  64.0 0.8 %copy.5 = bf16[128,2048]{1,0:T(8,128)(2,1)} copy(bf16[128,2048]{1,0:T(8,128)(2,1)S(1)} %tree_attention.1) | data formatting | bytes 1048576
Async XLA Ops:
  0.0 1.0 %copy-start = (bf16[128,2048]{1,0:T(8,128)(2,1)S(1)}, bf16[128,2048]{1,0:T(8,128)(2,1)}, u32[]{:S(2)}) copy-start(bf16[128,2048]{1,0:T(8,128)(2,1)} %q_in.1) | copy-start | bytes 1572868
  1.0 1.0 %copy-start.1 = (bf16[128,2048]{1,0:T(8,128)(2,1)S(1)}, bf16[128,2048]{1,0:T(8,128)(2,1)}, u32[]{:S(2)}) copy-start(bf16[128,2048]{1,0:T(8,128)(2,1)} %k_in.1) | copy-start | bytes 1572868
  2.1 1.0 %copy-start.2 = (bf16[128,2048]{1,0:T(8,128)(2,1)S(1)}, bf16[128,2048]{1,0:T(8,128)(2,1)}, u32[]{:S(2)}) copy-start(bf16[128,2048]{1,0:T(8,128)(2,1)} %v_in.1) | copy-start | bytes 1572868
where the time goes:
time: 65 us; the launch traced here: 64.8 us
  Pallas kernels  60.9 us (94%)
  local copies, waits for them, and re-layouts  3.92 us (6%)
    pallas_call x1, Pallas kernels, body(): pl.pallas_call(kernel, out_shape=jax.ShapeDtypeStruct(query_states.shape,...  60.9 us
    unnamed x7, local copies, waits for them, and re-layouts  3.92 us

commit v1 on v0

v1 whole, which is shorter than its diff:
```python
import math

import jax
import jax.numpy as jnp
from jax import lax
from jax.experimental import pallas as pl
from jax.experimental.pallas import tpu as pltpu
from jax.sharding import PartitionSpec as P

HEADS = 16
HALF = HEADS // 2
DIM = 128
LEAF = 128
CHIPS = 16
CHUNKS = 4
PER = HALF // CHUNKS
SCALE = 1.0 / math.sqrt(DIM)
SCALE2 = SCALE * math.log2(math.e)
MESH = pl.DeviceIdType.MESH
BF = jnp.bfloat16
F32 = jnp.float32


def nn(a, b):
    return lax.dot_general(a, b, (((1,), (0,)), ((), ())), preferred_element_type=F32)


def nt(a, b):
    return lax.dot_general(a, b, (((1,), (1,)), ((), ())), preferred_element_type=F32)


def grid_of(rows, columns):
    return (
        lax.broadcasted_iota(jnp.int32, (rows, columns), 0),
        lax.broadcasted_iota(jnp.int32, (rows, columns), 1),
    )


def halving(rows):
    i, j = grid_of(rows // 2, rows)
    return jnp.where((j >> 1) == i, 0.5, 0.0).astype(BF)


def halving_spread(rows, level):
    i, j = grid_of(rows, rows)
    first = (j & ((1 << (level - 1)) - 1)) == 0
    return jnp.where(((i >> level) == (j >> level)) & first, 0.5, 0.0).astype(BF)


def with_ones(values):
    return jnp.concatenate([values, jnp.ones_like(values)], axis=1)


def attend(scores, values):
    peak = jnp.max(scores[0], axis=1, keepdims=True)
    for s in scores[1:]:
        peak = jnp.maximum(peak, jnp.max(s, axis=1, keepdims=True))
    total = None
    for s, v in zip(scores, values):
        w = jnp.exp2((s - peak) * SCALE2).astype(BF)
        part = nn(w, with_ones(v))
        total = part if total is None else total + part
    den = total[:, DIM:]
    return total[:, :DIM] / den, peak, jnp.log(den)


def split3(x):
    high = x.astype(BF)
    rest = x - high.astype(F32)
    mid = rest.astype(BF)
    low = (rest - mid.astype(F32)).astype(BF)
    return jnp.concatenate([high, mid, low], axis=1)


def as_rows(eye, peak, total):
    return jnp.concatenate(
        [
            jnp.sum(jnp.where(eye, peak, 0.0), axis=0, keepdims=True),
            jnp.sum(jnp.where(eye, total, 0.0), axis=0, keepdims=True),
        ],
        axis=0,
    )


def spread_stats(pick3, stats):
    parts = split3(stats)
    both = nt(
        pick3,
        jnp.concatenate(
            [jnp.broadcast_to(parts[0:1], (DIM, 3 * DIM)), jnp.broadcast_to(parts[1:2], (DIM, 3 * DIM))],
            axis=0,
        ),
    )
    return both[:, :DIM], both[:, DIM:]


def kernel(
    q_in, k_in, v_in, out,
    full, near, kv1_s, kv1_r, q2_s, q2_r, kv2_s, kv2_r, far_s, far_r,
    kv4_s, kv5_s, kv6_s, kv4_r, kv5_r, kv6_r, q_up,
    res2_s, stat2_s, res2_r, stat2_r, res_s, stat_s, res_r, stat_r, done,
    load_sem, own_sem, near_ss, near_rs, kv1_ss, kv1_rs, q2_ss, q2_rs, kv2_ss, kv2_rs, far_ss, far_rs,
    up_ss, up_rs, res2_ss, res2_rs, stat2_ss, stat2_rs, res_ss, res_rs, stat_ss, stat_rs,
    out_ls, out_ss, out_rs,
):
    o = lax.axis_index("outer")
    n = lax.axis_index("inner")
    c = n % 2
    z = n // 2
    half = z // 8
    zl = z % 8
    quad = z // 4
    zq = z % 4
    gq = zq // 2
    zp = z % 2
    other = 1 - c
    differ = (half + c) % 2
    mate = (o, 2 * z + other)
    zs = z + 1 - 2 * zp
    o1 = o + 1 - 2 * (o % 2)
    o2 = o + 2 - 4 * ((o // 2) % 2)
    o3 = o2 + 1 - 2 * (o2 % 2)
    inputs = (q_in, k_in, v_in)

    def remote(src, dst, ss, rs, device):
        return pltpu.make_async_remote_copy(
            src_ref=src, dst_ref=dst, send_sem=ss, recv_sem=rs, device_id=device, device_id_type=MESH
        )

    def start_either(here, src, dst, ss, rs, device):
        @pl.when(here)
        def _():
            pltpu.make_async_copy(src, dst, rs).start()

        @pl.when(jnp.logical_not(here))
        def _():
            remote(src, dst, ss, rs, device).start()

    def end_either(here, src, dst, ss, rs, device):
        @pl.when(jnp.logical_not(here))
        def _():
            remote(src, dst, ss, rs, device).wait_send()

    def load(i, part):
        at = pl.ds(512 * part, 512)
        return pltpu.make_async_copy(inputs[i].at[:, at], full.at[i, :, at], load_sem.at[part, i])

    for part in range(4):
        for i in range(3):
            load(i, part).start()

    barrier = pltpu.get_barrier_semaphore()

    def greet(d):
        @pl.when(d != n)
        def _():
            pl.semaphore_signal(barrier, inc=1, device_id=(o, d), device_id_type=MESH)

    def greet_line(i, carry):
        greet(16 * c + i)
        return carry

    def greet_quad(i, carry):
        greet(8 * quad + i)
        return carry

    lax.fori_loop(0, 16, greet_line, 0)
    lax.fori_loop(0, 8, greet_quad, 0)
    for line in (o1, o2, o3):
        for cc in range(2):
            pl.semaphore_signal(barrier, inc=1, device_id=(line, 2 * z + cc), device_id_type=MESH)

    own = [
        pltpu.make_async_copy(
            inputs[i].at[:, pl.ds(1024 * c, 1024)], near.at[i, pl.ds(128 * c, 128), :], own_sem.at[i]
        )
        for i in range(3)
    ]
    for copy in own:
        copy.start()

    half128 = halving(128)
    half64 = halving(64)
    half32 = halving(32)

    for part in range(4):
        for i in range(3):
            load(i, part).wait()
        one = [nn(half128, full[i, :, part * 512 : (part + 1) * 512]).astype(BF) for i in range(3)]
        two = [nn(half64, x).astype(BF) for x in one]
        three = [nn(half32, x).astype(BF) for x in two]
        for u in range(4):
            h = part * 4 + u
            cut = slice(u * DIM, (u + 1) * DIM)
            kv1_s[h] = jnp.concatenate([one[1][:, cut], one[2][:, cut]], axis=1)
            q2_s[h] = two[0][:, cut]
            kv2_s[h] = jnp.concatenate([two[1][:, cut], two[2][:, cut]], axis=1)
            far_s[h] = jnp.concatenate([x[:, cut] for x in three], axis=1)

    pl.semaphore_wait(barrier, 28 + differ)

    mine = zl * 2 + c

    def far_route(k):
        step = (k + 1) // 2
        zz = (z + 16 + step * (2 * (k % 2) - 1)) % 16
        here = zz + 16 * differ == z
        return here, far_s.at[zz], far_r.at[mine], far_ss.at[k], far_rs.at[mine], (o, 2 * zz + half)

    def send_far(k, carry):
        start_either(*far_route(15 - k))
        return carry

    lax.fori_loop(0, 16, send_far, 0)

    place = 2 * zp + c

    def level2_routes(i):
        k = (zq + i) % 4
        chip = 4 * quad + k
        rows = pl.ds(32 * place, 32)
        heads = pl.ds(4 * k, 4)
        away = (k + 4 - zq) % 4
        return (
            (
                away + (gq + c) % 2 == 0,
                q2_s.at[heads], q2_r.at[:, rows, :], q2_ss.at[i], q2_rs.at[place], (o, 2 * chip + gq),
            ),
            (
                away + (gq + other) % 2 == 0,
                kv2_s.at[heads], kv2_r.at[:, rows, :], kv2_ss.at[i], kv2_rs.at[place], (o, 2 * chip + 1 - gq),
            ),
        )

    def send_level2(i, carry):
        for route in level2_routes(3 - i):
            start_either(*route)
        return carry

    lax.fori_loop(0, 4, send_level2, 0)

    near_copies = [
        remote(
            inputs[i].at[:, pl.ds(1024 * other, 1024)], near.at[i, pl.ds(128 * c, 128), :],
            near_ss.at[i], near_rs.at[i], mate,
        )
        for i in range(3)
    ]
    for copy in near_copies:
        copy.start()

    def kv1_copy(q, cc):
        return remote(
            kv1_s.at[pl.ds(HALF * cc + PER * q, PER)],
            kv1_r.at[pl.ds(PER * q, PER), pl.ds(64 * c, 64), :],
            kv1_ss.at[cc, q], kv1_rs.at[c, q], (o, 2 * zs + cc),
        )

    def send_kv1(q, carry):
        for cc in range(2):
            kv1_copy(q, cc).start()
        return carry

    lax.fori_loop(0, CHUNKS, send_kv1, 0)

    def wait_far(s, carry):
        remote(far_s.at[0], far_r.at[s], far_ss.at[0], far_rs.at[s], mate).wait_recv()
        return carry

    lax.fori_loop(0, 16, wait_far, 0)

    for g in range(2):
        kv3 = far_r[pl.ds(8 * g, 8), :, DIM:].reshape(128, 2 * DIM)
        kv4_s[pl.ds(64 * g, 64), :] = nn(half128, kv3).astype(BF)
    kv4_copy = remote(kv4_s, kv4_r, up_ss.at[0], up_rs.at[0], mate)
    kv4_copy.start()
    up = [kv4_copy]
    kv5 = nn(half128, kv4_s[...]).astype(BF)
    kv5_s[...] = kv5
    for cc in range(2):
        copy = remote(kv5_s, kv5_r.at[c], up_ss.at[1 + cc], up_rs.at[1 + c], (o1, 2 * z + cc))
        copy.start()
        up.append(copy)
    kv6_s[...] = nn(half64, kv5).astype(BF)
    slot = 2 * (o % 2) + c
    for k, line in enumerate((o2, o3)):
        for cc in range(2):
            copy = remote(
                kv6_s, kv6_r.at[slot], up_ss.at[3 + 2 * k + cc], up_rs.at[3 + slot], (line, 2 * z + cc)
            )
            copy.start()
            up.append(copy)

    spreads = [halving_spread(128, level) for level in range(1, 4)]
    for g in range(2):
        x = far_r[pl.ds(8 * g, 8), :, :DIM].reshape(128, DIM)
        for level in range(3):
            x = nn(spreads[level], x).astype(BF)
            q_up[level, g] = x

    eye_i, eye_j = grid_of(128, 128)
    eye = eye_i == eye_j

    for s in range(4):
        rows = pl.ds(32 * s, 32)
        remote(q2_s.at[pl.ds(0, 4)], q2_r.at[:, rows, :], q2_ss.at[0], q2_rs.at[s], mate).wait_recv()
        remote(kv2_s.at[pl.ds(0, 4)], kv2_r.at[:, rows, :], kv2_ss.at[0], kv2_rs.at[s], mate).wait_recv()
    for u in range(4):
        kv2 = kv2_r[u]
        result, peak, total = attend([nt(q2_r[u], kv2[:, :DIM])], [kv2[:, DIM:]])
        for i in range(2):
            res2_s[i, u] = result[64 * i : 64 * i + 64].astype(BF)
        stat2_s[u] = as_rows(eye, peak, total)

    def level2_results(i):
        k = 2 * c + i
        device = (o, 2 * (4 * quad + k) + gq)
        here = (k + 4 - zq) % 4 + (gq + c) % 2 == 0
        heads = pl.ds(4 * zp, 4)
        return (
            (here, res2_s.at[i], res2_r.at[heads], res2_ss.at[i], res2_rs.at[zp], device),
            (here, stat2_s, stat2_r.at[heads], stat2_ss.at[i], stat2_rs.at[zp], device),
        )

    for i in range(2):
        for route in level2_results(i):
            start_either(*route)

    kv4_copy.wait_recv()
    for cc in range(2):
        remote(kv5_s, kv5_r.at[cc], up_ss.at[1], up_rs.at[1 + cc], mate).wait_recv()
    for s in range(4):
        remote(kv6_s, kv6_r.at[s], up_ss.at[3], up_rs.at[3 + s], mate).wait_recv()

    def results(i):
        device = (o, 2 * (8 * c + i) + half)
        here = 8 * c + i + 16 * differ == z
        return (
            (here, res_s.at[i], res_r.at[zl], res_ss.at[i], res_rs.at[zl], device),
            (here, stat_s.at[i // 4], stat_r.at[zl], stat_ss.at[i], stat_rs.at[zl], device),
        )

    for g in range(2):
        keys = [
            far_r[pl.ds(8 * (1 - g), 8), :, DIM:].reshape(128, 2 * DIM),
            kv4_r[...],
            kv5_r[...].reshape(128, 2 * DIM),
            kv6_r[...].reshape(128, 2 * DIM),
        ]
        queries = [far_r[pl.ds(8 * g, 8), :, :DIM].reshape(128, DIM)] + [q_up[level, g] for level in range(3)]
        scores = [nt(q, kv[:, :DIM]) for q, kv in zip(queries, keys)]
        result, peak, total = attend(scores, [kv[:, DIM:] for kv in keys])
        for i in range(4):
            res_s[4 * g + i] = result[32 * i : 32 * i + 32].astype(BF)
        stat_s[g] = as_rows(eye, peak, total)
        for i in range(4 * g, 4 * g + 4):
            for route in results(i):
                start_either(*route)

    for copy in own:
        copy.wait()
    for i in range(3):
        remote(
            inputs[i].at[:, pl.ds(1024 * other, 1024)], near.at[i, pl.ds(128 * other, 128), :],
            near_ss.at[i], near_rs.at[i], mate,
        ).wait_recv()
    pairs = halving_spread(256, 1)

    def repeat_of(level):
        i, j = grid_of(256, 256 >> level)
        return jnp.where((i >> level) == j, 1.0, 0.0).astype(BF)

    def pick_of(level, first):
        i, j = grid_of(256, DIM)
        pick = jnp.where((i >> level) + first == j, 1.0, 0.0).astype(BF)
        return jnp.concatenate([pick, pick, pick], axis=1)

    repeat2, repeat3 = repeat_of(2), repeat_of(3)
    pick2, pick3 = pick_of(2, 64 * zp), pick_of(3, 32 * zq)

    def out_copies(j):
        at = pl.ds(pl.multiple_of((HALF * c + j) * DIM, DIM), DIM)
        return (
            pltpu.make_async_copy(done.at[j, pl.ds(128 * c, 128), :], out.at[:, at], out_ls.at[j]),
            remote(done.at[j, pl.ds(128 * other, 128), :], out.at[:, at], out_ss.at[j], out_rs.at[j], mate),
        )

    def near_step(q, carry):
        for cc in range(2):
            remote(
                kv1_s.at[pl.ds(0, PER)], kv1_r.at[pl.ds(PER * q, PER), pl.ds(64 * cc, 64), :],
                kv1_ss.at[0, q], kv1_rs.at[cc, q], mate,
            ).wait_recv()

        @pl.when(q % (CHUNKS // 2) == 0)
        def _():
            p = q // (CHUNKS // 2)
            heads = pl.ds(4 * p, 4)
            remote(res2_s.at[0], res2_r.at[heads], res2_ss.at[0], res2_rs.at[p], mate).wait_recv()
            remote(stat2_s, stat2_r.at[heads], stat2_ss.at[0], stat2_rs.at[p], mate).wait_recv()

        for u in range(PER):
            j = PER * q + u
            remote(res_s.at[0], res_r.at[j], res_ss.at[0], res_rs.at[j], mate).wait_recv()
            remote(stat_s.at[0], stat_r.at[j], stat_ss.at[0], stat_rs.at[j], mate).wait_recv()
        for u in range(PER):
            j = PER * q + u
            at = pl.ds(pl.multiple_of(j * DIM, DIM), DIM)
            x = near[0, :, at]
            x1 = nn(pairs, x).astype(BF)
            kv1 = kv1_r[j]
            scores = [nt(x, near[1, :, at]), nt(x1, kv1[:, :DIM])]
            fine, peak, total = attend(scores, [near[2, :, at], kv1[:, DIM:]])
            peak2, total2 = spread_stats(pick2, stat2_r[j])
            peak3, total3 = spread_stats(pick3, stat_r[j])
            gap2 = (peak2 - peak) * SCALE + (total2 - total)
            gap3 = (peak3 - peak) * SCALE + (total3 - total)
            top = jnp.maximum(jnp.maximum(gap2, gap3), 0.0)
            w1, w2, w3 = jnp.exp(-top), jnp.exp(gap2 - top), jnp.exp(gap3 - top)
            merged = w1 * fine + w2 * nn(repeat2, res2_r[j]) + w3 * nn(repeat3, res_r[j])
            done[j] = (merged / (w1 + w2 + w3)).astype(BF)
            for copy in out_copies(j):
                copy.start()
        return carry

    lax.fori_loop(0, CHUNKS, near_step, 0)

    def end_far(k, carry):
        end_either(*far_route(k))
        return carry

    lax.fori_loop(0, 16, end_far, 0)

    def end_level2(i, carry):
        for route in level2_routes(i):
            end_either(*route)
        return carry

    lax.fori_loop(0, 4, end_level2, 0)
    for copy in near_copies:
        copy.wait_send()

    def end_kv1(q, carry):
        for cc in range(2):
            kv1_copy(q, cc).wait_send()
        return carry

    lax.fori_loop(0, CHUNKS, end_kv1, 0)
    for copy in up:
        copy.wait_send()
    for i in range(2):
        for route in level2_results(i):
            end_either(*route)

    def end_results(i, carry):
        for route in results(i):
            end_either(*route)
        return carry

    lax.fori_loop(0, 8, end_results, 0)

    def end_out(j, carry):
        local, far = out_copies(j)
        local.wait()
        far.wait_send()
        at = pl.ds(pl.multiple_of((HALF * other + j) * DIM, DIM), DIM)
        remote(done.at[j, pl.ds(0, 128), :], out.at[:, at], out_ss.at[j], out_rs.at[j], mate).wait_recv()
        return carry

    lax.fori_loop(0, HALF, end_out, 0)


def body(query_states, key_states, value_states):
    dma = pltpu.SemaphoreType.DMA
    vmem = pltpu.VMEM
    return pl.pallas_call(
        kernel,
        out_shape=jax.ShapeDtypeStruct(query_states.shape, BF),
        in_specs=[pl.BlockSpec(memory_space=pl.ANY)] * 3,
        out_specs=pl.BlockSpec(memory_space=pl.ANY),
        scratch_shapes=[
            vmem((3, LEAF, HEADS * DIM), BF),
            vmem((3, 2 * LEAF, HALF * DIM), BF),
            vmem((HEADS, 64, 2 * DIM), BF),
            vmem((HALF, 128, 2 * DIM), BF),
            vmem((HEADS, 32, DIM), BF),
            vmem((4, 128, DIM), BF),
            vmem((HEADS, 32, 2 * DIM), BF),
            vmem((4, 128, 2 * DIM), BF),
            vmem((HEADS, 16, 3 * DIM), BF),
            vmem((CHIPS, 16, 3 * DIM), BF),
            vmem((128, 2 * DIM), BF),
            vmem((64, 2 * DIM), BF),
            vmem((32, 2 * DIM), BF),
            vmem((128, 2 * DIM), BF),
            vmem((2, 64, 2 * DIM), BF),
            vmem((4, 32, 2 * DIM), BF),
            vmem((3, 2, 128, DIM), BF),
            vmem((2, 4, 64, DIM), BF),
            vmem((4, 2, DIM), F32),
            vmem((8, 64, DIM), BF),
            vmem((8, 2, DIM), F32),
            vmem((8, 32, DIM), BF),
            vmem((2, 2, DIM), F32),
            vmem((8, 32, DIM), BF),
            vmem((8, 2, DIM), F32),
            vmem((HALF, 256, DIM), BF),
            dma((4, 3)), dma((3,)), dma((3,)), dma((3,)), dma((2, CHUNKS)), dma((2, CHUNKS)),
            dma((4,)), dma((4,)), dma((4,)), dma((4,)), dma((16,)), dma((16,)),
            dma((7,)), dma((7,)), dma((2,)), dma((2,)), dma((2,)), dma((2,)),
            dma((8,)), dma((8,)), dma((8,)), dma((8,)),
            dma((8,)), dma((8,)), dma((8,)),
        ],
        compiler_params=pltpu.CompilerParams(
            collective_id=0, has_side_effects=True, vmem_limit_bytes=60 * 1024 * 1024
        ),
        cost_estimate=pl.CostEstimate(flops=600_000_000, bytes_accessed=3_000_000, transcendentals=1_200_000),
        name="tree_attention",
    )(query_states, key_states, value_states)


def solution(mesh):
    placed = P(("outer", "inner"), None)
    return jax.shard_map(body, mesh=mesh, in_specs=(placed,) * 3, out_specs=placed, check_vma=False)
```

time: 65 us -> 60.2 us (0.926)
  the two profiles are of different devices: /device:TPU:11 before, /device:TPU:1 now
where the time goes in v1:
time: 60.2 us; the launch traced here: 60 us
  Pallas kernels  58.1 us (97%)
  local copies, waits for them, and re-layouts  1.88 us (3%)
    pallas_call x1, Pallas kernels, body(): pl.pallas_call(kernel, out_shape=jax.ShapeDtypeStruct(query_states.shape,...  58.1 us
    unnamed x1, local copies, waits for them, and re-layouts  1.88 us

profile of v1, /device:TPU:1, one launch (start us, length us, event | category | flops | bytes accessed | tf_op | source)
XLA Modules:
  0.0 60.0 jit_solution(9491683189893326585)
XLA Ops:
  0.0 58.1 %tree_attention.1 = bf16[128,2048]{1,0:T(8,128)(2,1)} custom-call(bf16[128,2048]{1,0:T(8,128)(2,1)} %q_in.1, bf16[128,2048]{1,0:T(8,128)(2,1)} %k_in.1, bf16[128,2048]{1,0:T(8,128)(2,1)} %v_in.1), custom_call_target="tpu_custom_call" | custom-call | flops 600000000 | bytes 3000000 | tf_op jit(solution)/shard_map/tree_attention/pallas_call | solution.py:476
  58.1 1.9 %copy.5 = bf16[128,2048]{1,0:T(8,128)(2,1)} copy(bf16[128,2048]{1,0:T(8,128)(2,1)} %tree_attention.1) | data formatting | bytes 1048576

commit v2 on v1

--- a/solution.py
+++ b/solution.py
@@ -97,7 +97,7 @@
 def kernel(
     q_in, k_in, v_in, out,
     full, near, kv1_s, kv1_r, q2_s, q2_r, kv2_s, kv2_r, far_s, far_r,
-    kv4_s, kv5_s, kv6_s, kv4_r, kv5_r, kv6_r, q_up,
+    kv4_s, kv5_s, kv6_s, kv4_r, kv5_r, kv6_r, q_up, near_o, near_m,
     res2_s, stat2_s, res2_r, stat2_r, res_s, stat_s, res_r, stat_r, done,
     load_sem, own_sem, near_ss, near_rs, kv1_ss, kv1_rs, q2_ss, q2_rs, kv2_ss, kv2_rs, far_ss, far_rs,
     up_ss, up_rs, res2_ss, res2_rs, stat2_ss, stat2_rs, res_ss, res_rs, stat_ss, stat_rs,
@@ -141,13 +141,15 @@
         def _():
             remote(src, dst, ss, rs, device).wait_send()
 
-    def load(i, part):
-        at = pl.ds(512 * part, 512)
-        return pltpu.make_async_copy(inputs[i].at[:, at], full.at[i, :, at], load_sem.at[part, i])
-
-    for part in range(4):
+    quarters = [(quad + shift) % 4 for shift in (2, 1, 3, 0)]
+
+    def load(i, step):
+        at = pl.ds(pl.multiple_of(512 * quarters[step], 512), 512)
+        return pltpu.make_async_copy(inputs[i].at[:, at], full.at[i, :, at], load_sem.at[step, i])
+
+    for step in range(4):
         for i in range(3):
-            load(i, part).start()
+            load(i, step).start()
 
     barrier = pltpu.get_barrier_semaphore()
 
@@ -183,40 +185,15 @@
     half64 = halving(64)
     half32 = halving(32)
 
-    for part in range(4):
-        for i in range(3):
-            load(i, part).wait()
-        one = [nn(half128, full[i, :, part * 512 : (part + 1) * 512]).astype(BF) for i in range(3)]
-        two = [nn(half64, x).astype(BF) for x in one]
-        three = [nn(half32, x).astype(BF) for x in two]
-        for u in range(4):
-            h = part * 4 + u
-            cut = slice(u * DIM, (u + 1) * DIM)
-            kv1_s[h] = jnp.concatenate([one[1][:, cut], one[2][:, cut]], axis=1)
-            q2_s[h] = two[0][:, cut]
-            kv2_s[h] = jnp.concatenate([two[1][:, cut], two[2][:, cut]], axis=1)
-            far_s[h] = jnp.concatenate([x[:, cut] for x in three], axis=1)
-
-    pl.semaphore_wait(barrier, 28 + differ)
-
     mine = zl * 2 + c
 
-    def far_route(k):
-        step = (k + 1) // 2
-        zz = (z + 16 + step * (2 * (k % 2) - 1)) % 16
+    def far_route(zz):
         here = zz + 16 * differ == z
-        return here, far_s.at[zz], far_r.at[mine], far_ss.at[k], far_rs.at[mine], (o, 2 * zz + half)
-
-    def send_far(k, carry):
-        start_either(*far_route(15 - k))
-        return carry
-
-    lax.fori_loop(0, 16, send_far, 0)
+        return here, far_s.at[zz], far_r.at[mine], far_ss.at[zz], far_rs.at[mine], (o, 2 * zz + half)
 
     place = 2 * zp + c
 
-    def level2_routes(i):
-        k = (zq + i) % 4
+    def level2_routes(k):
         chip = 4 * quad + k
         rows = pl.ds(32 * place, 32)
         heads = pl.ds(4 * k, 4)
@@ -224,20 +201,39 @@
         return (
             (
                 away + (gq + c) % 2 == 0,
-                q2_s.at[heads], q2_r.at[:, rows, :], q2_ss.at[i], q2_rs.at[place], (o, 2 * chip + gq),
+                q2_s.at[heads], q2_r.at[:, rows, :], q2_ss.at[k], q2_rs.at[place], (o, 2 * chip + gq),
             ),
             (
                 away + (gq + other) % 2 == 0,
-                kv2_s.at[heads], kv2_r.at[:, rows, :], kv2_ss.at[i], kv2_rs.at[place], (o, 2 * chip + 1 - gq),
+                kv2_s.at[heads], kv2_r.at[:, rows, :], kv2_ss.at[k], kv2_rs.at[place], (o, 2 * chip + 1 - gq),
             ),
         )
 
-    def send_level2(i, carry):
-        for route in level2_routes(3 - i):
+    for step in range(4):
+        part = quarters[step]
+        at = pl.ds(pl.multiple_of(512 * part, 512), 512)
+        for i in range(3):
+            load(i, step).wait()
+        one = [nn(half128, full[i, :, at]).astype(BF) for i in range(3)]
+        two = [nn(half64, x).astype(BF) for x in one]
+        three = [nn(half32, x).astype(BF) for x in two]
+        for u in range(4):
+            h = part * 4 + u
+            cut = slice(u * DIM, (u + 1) * DIM)
+            far_s[h] = jnp.concatenate([x[:, cut] for x in three], axis=1)
+            q2_s[h] = two[0][:, cut]
+            kv2_s[h] = jnp.concatenate([two[1][:, cut], two[2][:, cut]], axis=1)
+            kv1_s[h] = jnp.concatenate([one[1][:, cut], one[2][:, cut]], axis=1)
+        if step == 0:
+            pl.semaphore_wait(barrier, 28 + differ)
+
+        def send_far(u, carry):
+            start_either(*far_route(4 * part + u))
+            return carry
+
+        lax.fori_loop(0, 4, send_far, 0)
+        for route in level2_routes(part):
             start_either(*route)
-        return carry
-
-    lax.fori_loop(0, 4, send_level2, 0)
 
     near_copies = [
         remote(
@@ -262,6 +258,26 @@
         return carry
 
     lax.fori_loop(0, CHUNKS, send_kv1, 0)
+
+    for copy in own:
+        copy.wait()
+    for i in range(3):
+        remote(
+            inputs[i].at[:, pl.ds(1024 * other, 1024)], near.at[i, pl.ds(128 * other, 128), :],
+            near_ss.at[i], near_rs.at[i], mate,
+        ).wait_recv()
+
+    def level0(p, carry):
+        for u in range(2):
+            j = 2 * p + u
+            at = pl.ds(pl.multiple_of(j * DIM, DIM), DIM)
+            s = nt(near[0, :, at], near[1, :, at])
+            peak = jnp.max(s, axis=1, keepdims=True)
+            near_o[j] = nn(jnp.exp2((s - peak) * SCALE2).astype(BF), with_ones(near[2, :, at]))
+            near_m[j] = jnp.broadcast_to(peak, (256, DIM))
+        return carry
+
+    lax.fori_loop(0, HALF // 2, level0, 0)
 
     def wait_far(s, carry):
         remote(far_s.at[0], far_r.at[s], far_ss.at[0], far_rs.at[s], mate).wait_recv()
@@ -357,14 +373,31 @@
             for route in results(i):
                 start_either(*route)
 
-    for copy in own:
-        copy.wait()
-    for i in range(3):
-        remote(
-            inputs[i].at[:, pl.ds(1024 * other, 1024)], near.at[i, pl.ds(128 * other, 128), :],
-            near_ss.at[i], near_rs.at[i], mate,
-        ).wait_recv()
     pairs = halving_spread(256, 1)
+
+    def level1(q, carry):
+        for cc in range(2):
+            remote(
+                kv1_s.at[pl.ds(0, PER)], kv1_r.at[pl.ds(PER * q, PER), pl.ds(64 * cc, 64), :],
+                kv1_ss.at[0, q], kv1_rs.at[cc, q], mate,
+            ).wait_recv()
+        for u in range(PER):
+            j = PER * q + u
+            at = pl.ds(pl.multiple_of(j * DIM, DIM), DIM)
+            x1 = nn(pairs, near[0, :, at]).astype(BF)
+            kv1 = kv1_r[j]
+            s = nt(x1, kv1[:, :DIM])
+            old = near_m[j]
+            peak = jnp.maximum(old, jnp.max(s, axis=1, keepdims=True))
+            kept = jnp.exp2((old - peak) * SCALE2)
+            total = nn(jnp.exp2((s - peak) * SCALE2).astype(BF), with_ones(kv1[:, DIM:]))
+            den = kept * near_o[j, :, DIM:] + total[:, DIM:]
+            near_o[j, :, :DIM] = (kept * near_o[j, :, :DIM] + total[:, :DIM]) / den
+            near_o[j, :, DIM:] = jnp.log(den)
+            near_m[j] = peak
+        return carry
+
+    lax.fori_loop(0, CHUNKS, level1, 0)
 
     def repeat_of(level):
         i, j = grid_of(256, 256 >> level)
@@ -377,6 +410,30 @@
 
     repeat2, repeat3 = repeat_of(2), repeat_of(3)
     pick2, pick3 = pick_of(2, 64 * zp), pick_of(3, 32 * zq)
+
+    def merge2(p, carry):
+        @pl.when(p % 2 == 0)
+        def _():
+            k = p // 2
+            heads = pl.ds(4 * k, 4)
+            remote(res2_s.at[0], res2_r.at[heads], res2_ss.at[0], res2_rs.at[k], mate).wait_recv()
+            remote(stat2_s, stat2_r.at[heads], stat2_ss.at[0], stat2_rs.at[k], mate).wait_recv()
+
+        for u in range(2):
+            j = 2 * p + u
+            fine, total, peak = near_o[j, :, :DIM], near_o[j, :, DIM:], near_m[j]
+            coarse = nn(repeat2, res2_r[j])
+            peak2, total2 = spread_stats(pick2, stat2_r[j])
+            top = jnp.maximum(peak, peak2)
+            w1 = jnp.exp((peak - top) * SCALE + total)
+            w2 = jnp.exp((peak2 - top) * SCALE + total2)
+            both = w1 + w2
+            near_o[j, :, :DIM] = (w1 * fine + w2 * coarse) / both
+            near_o[j, :, DIM:] = jnp.log(both)
+            near_m[j] = top
+        return carry
+
+    lax.fori_loop(0, HALF // 2, merge2, 0)
 
     def out_copies(j):
         at = pl.ds(pl.multiple_of((HALF * c + j) * DIM, DIM), DIM)
@@ -385,45 +442,24 @@
             remote(done.at[j, pl.ds(128 * other, 128), :], out.at[:, at], out_ss.at[j], out_rs.at[j], mate),
         )
 
-    def near_step(q, carry):
-        for cc in range(2):
-            remote(
-                kv1_s.at[pl.ds(0, PER)], kv1_r.at[pl.ds(PER * q, PER), pl.ds(64 * cc, 64), :],
-                kv1_ss.at[0, q], kv1_rs.at[cc, q], mate,
-            ).wait_recv()
-
-        @pl.when(q % (CHUNKS // 2) == 0)
-        def _():
-            p = q // (CHUNKS // 2)
-            heads = pl.ds(4 * p, 4)
-            remote(res2_s.at[0], res2_r.at[heads], res2_ss.at[0], res2_rs.at[p], mate).wait_recv()
-            remote(stat2_s, stat2_r.at[heads], stat2_ss.at[0], stat2_rs.at[p], mate).wait_recv()
-
-        for u in range(PER):
-            j = PER * q + u
+    def merge3(p, carry):
+        for u in range(2):
+            j = 2 * p + u
             remote(res_s.at[0], res_r.at[j], res_ss.at[0], res_rs.at[j], mate).wait_recv()
             remote(stat_s.at[0], stat_r.at[j], stat_ss.at[0], stat_rs.at[j], mate).wait_recv()
-        for u in range(PER):
-            j = PER * q + u
-            at = pl.ds(pl.multiple_of(j * DIM, DIM), DIM)
-            x = near[0, :, at]
-            x1 = nn(pairs, x).astype(BF)
-            kv1 = kv1_r[j]
-            scores = [nt(x, near[1, :, at]), nt(x1, kv1[:, :DIM])]
-            fine, peak, total = attend(scores, [near[2, :, at], kv1[:, DIM:]])
-            peak2, total2 = spread_stats(pick2, stat2_r[j])
+        for u in range(2):
+            j = 2 * p + u
+            fine, total, peak = near_o[j, :, :DIM], near_o[j, :, DIM:], near_m[j]
+            coarse = nn(repeat3, res_r[j])
             peak3, total3 = spread_stats(pick3, stat_r[j])
-            gap2 = (peak2 - peak) * SCALE + (total2 - total)
-            gap3 = (peak3 - peak) * SCALE + (total3 - total)
-            top = jnp.maximum(jnp.maximum(gap2, gap3), 0.0)
-            w1, w2, w3 = jnp.exp(-top), jnp.exp(gap2 - top), jnp.exp(gap3 - top)
-            merged = w1 * fine + w2 * nn(repeat2, res2_r[j]) + w3 * nn(repeat3, res_r[j])
-            done[j] = (merged / (w1 + w2 + w3)).astype(BF)
+            gap = (peak3 - peak) * SCALE + (total3 - total)
+            share = 1.0 / (1.0 + jnp.exp(-gap))
+            done[j] = (fine + share * (coarse - fine)).astype(BF)
             for copy in out_copies(j):
                 copy.start()
         return carry
 
-    lax.fori_loop(0, CHUNKS, near_step, 0)
+    lax.fori_loop(0, HALF // 2, merge3, 0)
 
     def end_far(k, carry):
         end_either(*far_route(k))
@@ -476,7 +512,7 @@
     return pl.pallas_call(
         kernel,
         out_shape=jax.ShapeDtypeStruct(query_states.shape, BF),
-        in_specs=[pl.BlockSpec(memory_space=pl.ANY)] * 3,
+        in_specs=[pl.BlockSpec(memory_space=pltpu.HBM)] * 3,
         out_specs=pl.BlockSpec(memory_space=pl.ANY),
         scratch_shapes=[
             vmem((3, LEAF, HEADS * DIM), BF),
@@ -496,6 +532,8 @@
             vmem((2, 64, 2 * DIM), BF),
             vmem((4, 32, 2 * DIM), BF),
             vmem((3, 2, 128, DIM), BF),
+            vmem((HALF, 256, 2 * DIM), F32),
+            vmem((HALF, 256, DIM), F32),
             vmem((2, 4, 64, DIM), BF),
             vmem((4, 2, DIM), F32),
             vmem((8, 64, DIM), BF),
@@ -512,11 +550,11 @@
             dma((8,)), dma((8,)), dma((8,)),
         ],
         compiler_params=pltpu.CompilerParams(
-            collective_id=0, has_side_effects=True, vmem_limit_bytes=60 * 1024 * 1024
+            collective_id=0, has_side_effects=True, vmem_limit_bytes=40 * 1024 * 1024
         ),
         cost_estimate=pl.CostEstimate(flops=600_000_000, bytes_accessed=3_000_000, transcendentals=1_200_000),
         name="tree_attention",
-    )(query_states, key_states, value_states)
+    )(*(pltpu.with_memory_space_constraint(x, pltpu.HBM) for x in (query_states, key_states, value_states)))
 
 
 def solution(mesh):

time: 60.2 us -> 56.2 us (0.934)
  Pallas kernels: 58.1 us -> 55.2 us
  local copies, waits for them, and re-layouts: 1.88 us -> 0.8 us
    pallas_call x1, Pallas kernels: 58.1 us -> 55.2 us  [body(): pl.pallas_call(kernel, out_shape=jax.ShapeDtypeStruct(query_states.shape,...]
    unnamed x1, local copies, waits for them, and re-layouts: 1.88 us -> 0.8 us
where the time goes in v2:
time: 56.2 us; the launch traced here: 56 us
  Pallas kernels  55.2 us (98%)
  local copies, waits for them, and re-layouts  0.8 us (1%)
    pallas_call x1, Pallas kernels, body(): pl.pallas_call(kernel, out_shape=jax.ShapeDtypeStruct(query_states.shape,...  55.2 us

profile of v2, /device:TPU:1, one launch (start us, length us, event | category | flops | bytes accessed | tf_op | source)
XLA Modules:
  0.0 56.0 jit_solution(14748480907961506664)
XLA Ops:
  0.0 55.2 %tree_attention.1 = bf16[128,2048]{1,0:T(8,128)(2,1)S(1)} custom-call(bf16[128,2048]{1,0:T(8,128)(2,1)} %q_in.1, bf16[128,2048]{1,0:T(8,128)(2,1)} %k_in.1, bf16[128,2048]{1,0:T(8,128)(2,1)} %v_in.1), custom_call_target="tpu_custom_call" | custom-call | flops 600000000 | bytes 3000000 | tf_op jit(solution)/shard_map/tree_attention/pallas_call | solution.py:512
  55.2 0.8 %copy.5 = bf16[128,2048]{1,0:T(8,128)(2,1)} copy(bf16[128,2048]{1,0:T(8,128)(2,1)S(1)} %tree_attention.1) | data formatting | bytes 1048576

commit v3 on v2

--- a/solution.py
+++ b/solution.py
@@ -317,31 +317,6 @@
     eye_i, eye_j = grid_of(128, 128)
     eye = eye_i == eye_j
 
-    for s in range(4):
-        rows = pl.ds(32 * s, 32)
-        remote(q2_s.at[pl.ds(0, 4)], q2_r.at[:, rows, :], q2_ss.at[0], q2_rs.at[s], mate).wait_recv()
-        remote(kv2_s.at[pl.ds(0, 4)], kv2_r.at[:, rows, :], kv2_ss.at[0], kv2_rs.at[s], mate).wait_recv()
-    for u in range(4):
-        kv2 = kv2_r[u]
-        result, peak, total = attend([nt(q2_r[u], kv2[:, :DIM])], [kv2[:, DIM:]])
-        for i in range(2):
-            res2_s[i, u] = result[64 * i : 64 * i + 64].astype(BF)
-        stat2_s[u] = as_rows(eye, peak, total)
-
-    def level2_results(i):
-        k = 2 * c + i
-        device = (o, 2 * (4 * quad + k) + gq)
-        here = (k + 4 - zq) % 4 + (gq + c) % 2 == 0
-        heads = pl.ds(4 * zp, 4)
-        return (
-            (here, res2_s.at[i], res2_r.at[heads], res2_ss.at[i], res2_rs.at[zp], device),
-            (here, stat2_s, stat2_r.at[heads], stat2_ss.at[i], stat2_rs.at[zp], device),
-        )
-
-    for i in range(2):
-        for route in level2_results(i):
-            start_either(*route)
-
     kv4_copy.wait_recv()
     for cc in range(2):
         remote(kv5_s, kv5_r.at[cc], up_ss.at[1], up_rs.at[1 + cc], mate).wait_recv()
@@ -372,6 +347,31 @@
         for i in range(4 * g, 4 * g + 4):
             for route in results(i):
                 start_either(*route)
+
+    for s in range(4):
+        rows = pl.ds(32 * s, 32)
+        remote(q2_s.at[pl.ds(0, 4)], q2_r.at[:, rows, :], q2_ss.at[0], q2_rs.at[s], mate).wait_recv()
+        remote(kv2_s.at[pl.ds(0, 4)], kv2_r.at[:, rows, :], kv2_ss.at[0], kv2_rs.at[s], mate).wait_recv()
+    for u in range(4):
+        kv2 = kv2_r[u]
+        result, peak, total = attend([nt(q2_r[u], kv2[:, :DIM])], [kv2[:, DIM:]])
+        for i in range(2):
+            res2_s[i, u] = result[64 * i : 64 * i + 64].astype(BF)
+        stat2_s[u] = as_rows(eye, peak, total)
+
+    def level2_results(i):
+        k = 2 * c + i
+        device = (o, 2 * (4 * quad + k) + gq)
+        here = (k + 4 - zq) % 4 + (gq + c) % 2 == 0
+        heads = pl.ds(4 * zp, 4)
+        return (
+            (here, res2_s.at[i], res2_r.at[heads], res2_ss.at[i], res2_rs.at[zp], device),
+            (here, stat2_s, stat2_r.at[heads], stat2_ss.at[i], stat2_rs.at[zp], device),
+        )
+
+    for i in range(2):
+        for route in level2_results(i):
+            start_either(*route)
 
     pairs = halving_spread(256, 1)
 
@@ -442,24 +442,18 @@
             remote(done.at[j, pl.ds(128 * other, 128), :], out.at[:, at], out_ss.at[j], out_rs.at[j], mate),
         )
 
-    def merge3(p, carry):
-        for u in range(2):
-            j = 2 * p + u
-            remote(res_s.at[0], res_r.at[j], res_ss.at[0], res_rs.at[j], mate).wait_recv()
-            remote(stat_s.at[0], stat_r.at[j], stat_ss.at[0], stat_rs.at[j], mate).wait_recv()
-        for u in range(2):
-            j = 2 * p + u
-            fine, total, peak = near_o[j, :, :DIM], near_o[j, :, DIM:], near_m[j]
-            coarse = nn(repeat3, res_r[j])
-            peak3, total3 = spread_stats(pick3, stat_r[j])
-            gap = (peak3 - peak) * SCALE + (total3 - total)
-            share = 1.0 / (1.0 + jnp.exp(-gap))
-            done[j] = (fine + share * (coarse - fine)).astype(BF)
-            for copy in out_copies(j):
-                copy.start()
-        return carry
-
-    lax.fori_loop(0, HALF // 2, merge3, 0)
+    for j in range(HALF):
+        remote(res_s.at[0], res_r.at[j], res_ss.at[0], res_rs.at[j], mate).wait_recv()
+        remote(stat_s.at[0], stat_r.at[j], stat_ss.at[0], stat_rs.at[j], mate).wait_recv()
+    columns = nt(pick3, split3(jnp.concatenate([stat_r[j] for j in range(HALF)], axis=0)))
+    for j in range(HALF):
+        fine, total, peak = near_o[j, :, :DIM], near_o[j, :, DIM:], near_m[j]
+        peak3, total3 = columns[:, 2 * j : 2 * j + 1], columns[:, 2 * j + 1 : 2 * j + 2]
+        gap = (peak3 - peak) * SCALE + (total3 - total)
+        share = 1.0 / (1.0 + jnp.exp(-gap))
+        done[j] = (fine + share * (nn(repeat3, res_r[j]) - fine)).astype(BF)
+        for copy in out_copies(j):
+            copy.start()
 
     def end_far(k, carry):
         end_either(*far_route(k))

time: 56.2 us -> 54.9 us (0.977)
  Pallas kernels: 55.2 us -> 54 us
    pallas_call x1, Pallas kernels: 55.2 us -> 54 us  [body(): pl.pallas_call(kernel, out_shape=jax.ShapeDtypeStruct(query_states.shape,...]
where the time goes in v3:
time: 54.9 us; the launch traced here: 54.8 us
  Pallas kernels  54 us (98%)
  local copies, waits for them, and re-layouts  0.8 us (1%)
    pallas_call x1, Pallas kernels, body(): pl.pallas_call(kernel, out_shape=jax.ShapeDtypeStruct(query_states.shape,...  54 us

profile of v3, /device:TPU:1, one launch (start us, length us, event | category | flops | bytes accessed | tf_op | source)
XLA Modules:
  0.0 54.8 jit_solution(11580478142953324196)
XLA Ops:
  0.0 54.0 %tree_attention.1 = bf16[128,2048]{1,0:T(8,128)(2,1)S(1)} custom-call(bf16[128,2048]{1,0:T(8,128)(2,1)} %q_in.1, bf16[128,2048]{1,0:T(8,128)(2,1)} %k_in.1, bf16[128,2048]{1,0:T(8,128)(2,1)} %v_in.1), custom_call_target="tpu_custom_call" | custom-call | flops 600000000 | bytes 3000000 | tf_op jit(solution)/shard_map/tree_attention/pallas_call | solution.py:506
  54.0 0.8 %copy.5 = bf16[128,2048]{1,0:T(8,128)(2,1)} copy(bf16[128,2048]{1,0:T(8,128)(2,1)S(1)} %tree_attention.1) | data formatting | bytes 1048576

commit v4 on v3

--- a/solution.py
+++ b/solution.py
@@ -147,10 +147,6 @@
         at = pl.ds(pl.multiple_of(512 * quarters[step], 512), 512)
         return pltpu.make_async_copy(inputs[i].at[:, at], full.at[i, :, at], load_sem.at[step, i])
 
-    for step in range(4):
-        for i in range(3):
-            load(i, step).start()
-
     barrier = pltpu.get_barrier_semaphore()
 
     def greet(d):
@@ -178,8 +174,9 @@
         )
         for i in range(3)
     ]
-    for copy in own:
-        copy.start()
+    for step in range(4):
+        for i in range(3):
+            load(i, step).start()
 
     half128 = halving(128)
     half64 = halving(64)
@@ -242,6 +239,9 @@
         )
         for i in range(3)
     ]
+    for copy in own:
+        copy.start()
+
     for copy in near_copies:
         copy.start()
 
@@ -411,29 +411,21 @@
     repeat2, repeat3 = repeat_of(2), repeat_of(3)
     pick2, pick3 = pick_of(2, 64 * zp), pick_of(3, 32 * zq)
 
-    def merge2(p, carry):
-        @pl.when(p % 2 == 0)
-        def _():
-            k = p // 2
-            heads = pl.ds(4 * k, 4)
-            remote(res2_s.at[0], res2_r.at[heads], res2_ss.at[0], res2_rs.at[k], mate).wait_recv()
-            remote(stat2_s, stat2_r.at[heads], stat2_ss.at[0], stat2_rs.at[k], mate).wait_recv()
-
-        for u in range(2):
-            j = 2 * p + u
-            fine, total, peak = near_o[j, :, :DIM], near_o[j, :, DIM:], near_m[j]
-            coarse = nn(repeat2, res2_r[j])
-            peak2, total2 = spread_stats(pick2, stat2_r[j])
-            top = jnp.maximum(peak, peak2)
-            w1 = jnp.exp((peak - top) * SCALE + total)
-            w2 = jnp.exp((peak2 - top) * SCALE + total2)
-            both = w1 + w2
-            near_o[j, :, :DIM] = (w1 * fine + w2 * coarse) / both
-            near_o[j, :, DIM:] = jnp.log(both)
-            near_m[j] = top
-        return carry
-
-    lax.fori_loop(0, HALF // 2, merge2, 0)
+    for k in range(2):
+        heads = pl.ds(4 * k, 4)
+        remote(res2_s.at[0], res2_r.at[heads], res2_ss.at[0], res2_rs.at[k], mate).wait_recv()
+        remote(stat2_s, stat2_r.at[heads], stat2_ss.at[0], stat2_rs.at[k], mate).wait_recv()
+    columns = nt(pick2, split3(jnp.concatenate([stat2_r[j] for j in range(HALF)], axis=0)))
+    for j in range(HALF):
+        fine, total, peak = near_o[j, :, :DIM], near_o[j, :, DIM:], near_m[j]
+        peak2, total2 = columns[:, 2 * j : 2 * j + 1], columns[:, 2 * j + 1 : 2 * j + 2]
+        top = jnp.maximum(peak, peak2)
+        w1 = jnp.exp((peak - top) * SCALE + total)
+        w2 = jnp.exp((peak2 - top) * SCALE + total2)
+        both = w1 + w2
+        near_o[j, :, :DIM] = (w1 * fine + w2 * nn(repeat2, res2_r[j])) / both
+        near_o[j, :, DIM:] = jnp.log(both)
+        near_m[j] = top
 
     def out_copies(j):
         at = pl.ds(pl.multiple_of((HALF * c + j) * DIM, DIM), DIM)
@@ -452,7 +444,7 @@
         gap = (peak3 - peak) * SCALE + (total3 - total)
         share = 1.0 / (1.0 + jnp.exp(-gap))
         done[j] = (fine + share * (nn(repeat3, res_r[j]) - fine)).astype(BF)
-        for copy in out_copies(j):
+        for copy in reversed(out_copies(j)):
             copy.start()
 
     def end_far(k, carry):

time: 54.9 us -> 54.8 us (level)
  no operation moved by 1% of the time
where the time goes in v4:
time: 54.8 us; the launch traced here: 54.7 us
  Pallas kernels  53.9 us (98%)
  local copies, waits for them, and re-layouts  0.8 us (1%)
    pallas_call x1, Pallas kernels, body(): pl.pallas_call(kernel, out_shape=jax.ShapeDtypeStruct(query_states.shape,...  53.9 us

profile of v4, /device:TPU:1, one launch (start us, length us, event | category | flops | bytes accessed | tf_op | source)
XLA Modules:
  0.0 54.7 jit_solution(14869741429338104451)
XLA Ops:
  0.0 53.9 %tree_attention.1 = bf16[128,2048]{1,0:T(8,128)(2,1)S(1)} custom-call(bf16[128,2048]{1,0:T(8,128)(2,1)} %q_in.1, bf16[128,2048]{1,0:T(8,128)(2,1)} %k_in.1, bf16[128,2048]{1,0:T(8,128)(2,1)} %v_in.1), custom_call_target="tpu_custom_call" | custom-call | flops 600000000 | bytes 3000000 | tf_op jit(solution)/shard_map/tree_attention/pallas_call | solution.py:498
  53.9 0.8 %copy.5 = bf16[128,2048]{1,0:T(8,128)(2,1)} copy(bf16[128,2048]{1,0:T(8,128)(2,1)S(1)} %tree_attention.1) | data formatting | bytes 1048576
